TPU v7x, 512 devices: a whole 4x4x16 slice. The times are simulated.
512 devices in a mesh: space: 32 (over x, y, core), mode: 16 (over z).
Axes of the slice: x: 4, y: 4, z: 16, core: 2. Of those that a mesh axis runs over, the one named last changes fastest.
Arguments:
- basis: bfloat16 [32, 5, 65536], P('mode', None, 'space'), may hold values from -144 to 144
- jacobian: bfloat16 [3, 5, 5, 65536], P(None, None, None, 'space'), may hold values from -1.5 to 1.5
- sample_list: int32 [32, 64], P('space'), may hold values from 0 to 511, as said below
- sample_weight: float32 [32, 64], P('space'), may hold values from 0.25 to 2
Outputs:
- update: float32 [32, 5, 65536], P('mode', None, 'space')
Inputs may be any that keep to these rules, and one draw needn't show every extreme that they name: `sample_list`: row o holds 64 different tile numbers: exactly 4 from each of 16 different devices (device s holds tiles 16 * s to 16 * s + 15), one of which is device o itself, whose first and last tiles are in the row.
All inputs are finite; a program needn't handle non-finite values.
Results may differ from a plain program's by a relative error of at most 0.005.
Values may be sent and summed in bfloat16 or wider, within the bound.
A program may use at most 64 MiB of HBM per device.

v0:
```python
import jax
import jax.numpy as jnp
from jax import lax
from jax.sharding import PartitionSpec as P

F = 5
PANEL = 32
TILE = 128
CAP = 4


def extended(cells, sides, width):
    for axis, dim in sides:
        count = lax.axis_size(axis)
        ends = count - 1
        head = lax.slice_in_dim(cells, 0, width, axis=dim)
        tail = lax.slice_in_dim(cells, cells.shape[dim] - width, cells.shape[dim], axis=dim)
        cells = jnp.concatenate(
            [
                lax.ppermute(tail, axis, [(i, (i + 1) % count) for i in range(ends)]),
                cells,
                lax.ppermute(head, axis, [((i + 1) % count, i) for i in range(ends)]),
            ],
            axis=dim,
        )
    return cells


def passed_along(block, axis, distance):
    devices = range(lax.axis_size(axis))
    route = [(i - distance, i) for i in devices if i - distance in devices]
    return lax.ppermute(block, axis, route)


def slot_layout(tile_ids, tiles_here):
    source = tile_ids // tiles_here
    local_tile = tile_ids - source * tiles_here
    entry_order = jnp.arange(tile_ids.shape[-1])
    earlier = entry_order[None, :] < entry_order[:, None]
    matched = (source[..., :, None] == source[..., None, :]) & earlier
    slot_rank = jnp.sum(matched.astype(jnp.int32), axis=-1)
    return (source, local_tile, slot_rank)


def transpose_apply(neighbor_link, quadrature_weight):
    return jnp.sum(neighbor_link[None, :, :, :] * quadrature_weight[:, :, None, :], axis=1)


def shards(basis, jacobian, sample_list, sample_weight):
    space_count = lax.axis_size("space")
    modes_here, fields, cells = basis.shape
    tiles_here = cells // TILE
    capacity = CAP
    rimmed = extended(basis, (("space", 2),), 1)
    western_cells = rimmed[:, :, :-2]
    eastern_cells = rimmed[:, :, 2:]
    operator_result = jnp.einsum(
        "wvt,zvt->zwt", jacobian[0], basis, preferred_element_type=jnp.float32
    )
    operator_result = operator_result + jnp.einsum(
        "wvt,zvt->zwt", jacobian[1], western_cells, preferred_element_type=jnp.float32
    )
    operator_result = operator_result + jnp.einsum(
        "wvt,zvt->zwt", jacobian[2], eastern_cells, preferred_element_type=jnp.float32
    )
    operator_result = operator_result.astype(jnp.bfloat16)
    source, local_tile, slot_rank = slot_layout(sample_list, tiles_here)
    slot_index = (source * capacity + slot_rank)[0]
    places = jnp.arange(space_count * capacity)
    onehot = slot_index[:, None] == places[None, :]
    position_weight = jnp.sum(jnp.where(onehot, sample_weight[0][:, None], 0.0), axis=0)
    wanted_here = jnp.sum(jnp.where(onehot, local_tile[0][:, None] + 1, 0), axis=0) - 1
    asked = lax.all_to_all(
        wanted_here.reshape(space_count, capacity), "space", split_axis=0, concat_axis=0, tiled=True
    )
    selector = (asked.reshape(-1)[:, None] == jnp.arange(tiles_here)[None, :]).astype(jnp.bfloat16)
    tile_view = operator_result.reshape(modes_here, fields, tiles_here, TILE)
    outgoing = jnp.einsum(
        "sk,pfkc->pfsc", selector, tile_view, preferred_element_type=jnp.float32
    ).astype(jnp.bfloat16)
    outgoing = outgoing.reshape(modes_here, fields, space_count, capacity, TILE)
    incoming_rows = lax.all_to_all(outgoing, "space", split_axis=2, concat_axis=2, tiled=True)
    incoming_rows = incoming_rows.reshape(modes_here, fields, space_count * capacity, TILE)
    sample_rows = jnp.einsum(
        "ugeb,e->ugb", incoming_rows, position_weight, preferred_element_type=jnp.float32
    )
    partial_square = jnp.sum(sample_rows * sample_rows, axis=(0, 1))
    total_square = lax.psum(partial_square, "mode")
    normalized = sample_rows * lax.rsqrt(total_square / (PANEL * F) + 1e-05)[None, None, :]
    scaled = (
        position_weight.reshape(space_count, capacity)[None, None, :, :, None]
        * normalized[:, :, None, None, :]
    ).astype(jnp.bfloat16)
    scaled_back = lax.all_to_all(scaled, "space", split_axis=2, concat_axis=2, tiled=True)
    scaled_back = scaled_back.reshape(modes_here, fields, space_count * capacity, TILE)
    returned = jnp.einsum(
        "sk,pfsc->pfkc", selector, scaled_back, preferred_element_type=jnp.float32
    )
    returned = returned.reshape(modes_here, fields, cells)
    center_stencil = transpose_apply(jacobian[0], returned)
    below_stencil = transpose_apply(jacobian[1], returned)
    above_stencil = transpose_apply(jacobian[2], returned)
    from_next = passed_along(below_stencil[:, :, :1], "space", -1)
    from_prev = passed_along(above_stencil[:, :, -1:], "space", 1)
    update = basis.astype(jnp.float32) + center_stencil
    update = update + jnp.concatenate([below_stencil[:, :, 1:], from_next], axis=2)
    update = update + jnp.concatenate([from_prev, above_stencil[:, :, :-1]], axis=2)
    return update


def solution(mesh):
    placed = (
        P("mode", None, "space"),
        P(None, None, None, "space"),
        P("space", None),
        P("space", None),
    )
    return jax.shard_map(
        shards, mesh=mesh, in_specs=placed, out_specs=P("mode", None, "space"), check_vma=False
    )
```

profile of v0, /device:TPU:1, one launch (start us, length us, event | category | flops | bytes accessed | tf_op | source)
XLA Modules:
  0.0 145.8 jit_solution(10601634594347178904)
XLA Ops:
  0.8 8.8 %collective-permute-start.1 = (bf16[2,5,1]{2,0,1:T(2,128)(2,1)S(1)}, bf16[2,5,1]{2,0,1:T(2,128)(2,1)S(1)}, u32[]{:S(2)}, u32[]{:S(2)}) collective-permute-start(bf16[2,5,1]{2,0,1:T(2,128)(2,1)S(1)} %get-tuple-element.15), channel_id=1, source_target_pairs={{16,0},{32,16},{48,32},{64,48},{80,64},{96,80},{112,96},{128,112},... | collective-permute-start | bytes 68 | tf_op jit(solution)/shard_map/ppermute | solution.py:22
  9.6 1.9 %collective-permute-start = (bf16[2,5,1]{2,0,1:T(2,128)(2,1)S(1)}, bf16[2,5,1]{2,0,1:T(2,128)(2,1)S(1)}, u32[]{:S(2)}, u32[]{:S(2)}) collective-permute-start(bf16[2,5,1]{2,0,1:T(2,128)(2,1)S(1)} %get-tuple-element.16), channel_id=1, source_target_pairs={{0,16},{16,32},{32,48},{48,64},{64,80},{80,96},{96,112},{112,128},... | collective-permute-start | bytes 68 | tf_op jit(solution)/shard_map/ppermute | solution.py:20
  13.2 4.8 %all-to-all-start = ((s32[32,1,4]{2,1,0:T(1,128)}), s32[32,1,4]{2,1,0:T(1,128)S(1)}, u32[]{:S(2)}, u32[]{:S(2)}) async-start(s32[32,1,4]{2,1,0:T(1,128)} %bitcast.10), calls=%async_computation | async-start | bytes 32768 | tf_op jit(solution)/shard_map/all_to_all | solution.py:73
  18.0 2.1 %copy.64 = bf16[2,5,2048]{1,0,2:T(2,128)(2,1)S(1)} copy(bf16[2,5,2048]{2,0,1:T(2,128)(2,1)} %param.4) | data formatting | bytes 81920 | tf_op args[0]
  20.9 2.0 %fusion.20 = (bf16[1,5,5,2048]{3,0,2,1:T(2,128)(2,1)S(1)}, bf16[1,5,5,2048]{3,0,2,1:T(2,128)(2,1)S(1)}, bf16[1,5,5,2048]{3,0,2,1:T(2,128)(2,1)S(1)}) fusion(bf16[3,5,5,2048]{3,0,2,1:T(4,128)(2,1)} %param.5), kind=kLoop, calls=%fused_computation.44 | loop fusion | bytes 614400 | tf_op jit(solution)/shard_map/slice | solution.py:64
  23.0 4.0 %copy.82 = bf16[1,5,5,2048]{2,1,3,0:T(8,128)(2,1)} copy(bf16[1,5,5,2048]{3,0,2,1:T(2,128)(2,1)S(1)} %get-tuple-element.10) | data formatting | bytes 204800
  27.0 4.0 %copy.81 = bf16[1,5,5,2048]{2,1,3,0:T(8,128)(2,1)} copy(bf16[1,5,5,2048]{3,0,2,1:T(2,128)(2,1)S(1)} %get-tuple-element.11) | data formatting | bytes 204800
  31.0 4.0 %copy.80 = bf16[1,5,5,2048]{2,1,3,0:T(8,128)(2,1)} copy(bf16[1,5,5,2048]{3,0,2,1:T(2,128)(2,1)S(1)} %get-tuple-element.12) | data formatting | bytes 204800
  35.0 5.1 %bitcast_convert_fusion = f32[5,5,2048]{1,0,2:T(8,128)} fusion(bf16[1,5,5,2048]{2,1,3,0:T(8,128)(2,1)} %copy.82), kind=kLoop, calls=%fused_computation | loop fusion | flops 51200 | bytes 307200 | tf_op jit(solution)/shard_map/mul | solution.py:46
  40.1 4.8 %copy.76 = f32[5,5,2048]{2,1,0:T(8,128)S(1)} copy(f32[5,5,2048]{1,0,2:T(8,128)} %bitcast_convert_fusion) | data formatting | bytes 409600 | tf_op jit(solution)/shard_map/mul | solution.py:46
  44.9 5.9 %fusion.4 = f32[2048,2,5]{2,1,0:T(2,128)} fusion(bf16[2,5,2048]{1,0,2:T(2,128)(2,1)S(1)} %copy.64, bf16[1,5,5,2048]{2,1,3,0:T(8,128)(2,1)} %copy.80), kind=kOutput, calls=%fused_computation.6 | convolution fusion | flops 204800 | bytes 225280 | tf_op jit(solution)/shard_map/wvt,zvt->zwt/dot_general | solution.py:57
  50.9 0.9 copy.68
  52.8 4.6 %fusion.2 = f32[2048,2,5]{2,1,0:T(2,128)S(1)} fusion(bf16[2,5,2048]{1,0,2:T(2,128)(2,1)S(1)} %copy.66, bf16[1,5,5,2048]{2,1,3,0:T(8,128)(2,1)} %copy.81), kind=kOutput, calls=%fused_computation.4 | convolution fusion | flops 204800 | bytes 225280 | tf_op jit(solution)/shard_map/wvt,zvt->zwt/dot_general | solution.py:60
  57.5 2.4 %add_convert_fusion = bf16[2048,2,5]{2,1,0:T(2,128)(2,1)S(1)} fusion(f32[2048,2,5]{2,1,0:T(2,128)S(1)} %copy-done.2, f32[2048,2,5]{2,1,0:T(2,128)S(1)} %fusion.2, bf16[2,5,2048]{1,0,2:T(2,128)(2,1)S(1)} %copy.68, bf16[1,5,5,2048]{2,1,3,0:T(8,128)(2,1)S(1)} %copy-done), kind=kOutput, calls=%fused_computation.9 | convolution fusion | flops 266240 | bytes 348160 | tf_op jit(solution)/shard_map/wvt,zvt->zwt/dot_general | solution.py:63
  63.0 7.4 %all-to-all-start.1 = ((bf16[2,5,32,4,128]{4,3,1,0,2:T(4,128)(2,1)}), bf16[2,5,32,4,128]{4,3,1,0,2:T(4,128)(2,1)S(1)}, u32[]{:S(2)}, u32[]{:S(2)}) async-start(bf16[2,5,32,4,128]{4,3,1,0,2:T(4,128)(2,1)} %copy.71), calls=%async_computation.1 | async-start | bytes 655360 | tf_op jit(solution)/shard_map/all_to_all | solution.py:82
  70.4 5.1 %bitcast_convert_fusion.2 = f32[5,5,2048]{1,0,2:T(8,128)} fusion(bf16[1,5,5,2048]{2,1,3,0:T(8,128)(2,1)} %copy.80), kind=kLoop, calls=%fused_computation.8 | loop fusion | flops 51200 | bytes 307200 | tf_op jit(solution)/shard_map/mul | solution.py:46
  75.5 4.8 %copy.63 = f32[5,5,2048]{2,1,0:T(8,128)S(1)} copy(f32[5,5,2048]{1,0,2:T(8,128)} %bitcast_convert_fusion.2) | data formatting | bytes 409600 | tf_op jit(solution)/shard_map/mul | solution.py:46
  80.6 29.3 %psum.7 = f32[128]{0:T(128)S(1)} all-reduce(f32[128]{0:T(128)S(1)} %fusion.10), channel_id=1, replica_groups=mesh['space'=32,'mode'=16] {'mode'}, use_global_device_ids=true, to_apply=%region_4.5 | all-reduce | flops 128 | bytes 1024 | tf_op jit(solution)/shard_map/psum | solution.py:88
  110.8 14.6 %all-to-all-start.2 = ((bf16[2,5,32,4,128]{4,3,1,0,2:T(4,128)(2,1)}), bf16[2,5,32,4,128]{4,3,1,0,2:T(4,128)(2,1)S(1)}, u32[]{:S(2)}, u32[]{:S(2)}) async-start(bf16[2,5,32,4,128]{4,3,1,0,2:T(4,128)(2,1)} %multiply_convert_fusion), calls=%async_computation.2 | async-start | bytes 655360 | tf_op jit(solution)/shard_map/all_to_all | solution.py:94
  125.5 5.1 %bitcast_convert_fusion.1 = f32[5,5,2048]{1,0,2:T(8,128)} fusion(bf16[1,5,5,2048]{2,1,3,0:T(8,128)(2,1)} %copy.81), kind=kLoop, calls=%fused_computation.3 | loop fusion | flops 51200 | bytes 307200 | tf_op jit(solution)/shard_map/mul | solution.py:46
  130.5 4.8 %copy.75 = f32[5,5,2048]{2,1,0:T(8,128)S(1)} copy(f32[5,5,2048]{1,0,2:T(8,128)} %bitcast_convert_fusion.1) | data formatting | bytes 409600 | tf_op jit(solution)/shard_map/mul | solution.py:46
  136.5 3.5 %collective-permute-start.3 = (f32[2,5,1]{2,0,1:T(2,128)S(1)}, f32[2,5,1]{2,0,1:T(2,128)S(1)}, u32[]{:S(2)}, u32[]{:S(2)}) collective-permute-start(f32[2,5,1]{2,0,1:T(2,128)S(1)} %slice.51), channel_id=1, source_target_pairs={{0,16},{16,32},{32,48},{48,64},{64,80},{80,96},{96,112},{112,128},... | collective-permute-start | bytes 128 | tf_op jit(solution)/shard_map/ppermute | solution.py:32
  140.1 1.9 %collective-permute-start.2 = (f32[2,5,1]{2,0,1:T(2,128)S(1)}, f32[2,5,1]{2,0,1:T(2,128)S(1)}, u32[]{:S(2)}, u32[]{:S(2)}) collective-permute-start(f32[2,5,1]{2,0,1:T(2,128)S(1)} %slice.50), channel_id=1, source_target_pairs={{16,0},{32,16},{48,32},{64,48},{80,64},{96,80},{112,96},{128,112},... | collective-permute-start | bytes 128 | tf_op jit(solution)/shard_map/ppermute | solution.py:32
  142.0 3.0 %collective-permute-done.2 = f32[2,5,1]{2,0,1:T(2,128)S(1)} collective-permute-done((f32[2,5,1]{2,0,1:T(2,128)S(1)}, f32[2,5,1]{2,0,1:T(2,128)S(1)}, u32[]{:S(2)}, u32[]{:S(2)}) %collective-permute-start.2) | collective-permute-done | bytes 72 | tf_op jit(solution)/shard_map/ppermute | solution.py:32
  (44 shorter events, 10.7 us)
Async XLA Ops:
  0.8 49.9 %collective-permute-start.1 = (bf16[2,5,1]{2,0,1:T(2,128)(2,1)S(1)}, bf16[2,5,1]{2,0,1:T(2,128)(2,1)S(1)}, u32[]{:S(2)}, u32[]{:S(2)}) collective-permute-start(bf16[2,5,1]{2,0,1:T(2,128)(2,1)S(1)} %get-tuple-element.15), channel_id=1, source_target_pairs={{16,0},{32,16},{48,32},{64,48},{80,64},{96,80},{112,96},{128,112},... | collective-permute-start | bytes 68 | tf_op jit(solution)/shard_map/ppermute | solution.py:22
  9.6 41.2 %collective-permute-start = (bf16[2,5,1]{2,0,1:T(2,128)(2,1)S(1)}, bf16[2,5,1]{2,0,1:T(2,128)(2,1)S(1)}, u32[]{:S(2)}, u32[]{:S(2)}) collective-permute-start(bf16[2,5,1]{2,0,1:T(2,128)(2,1)S(1)} %get-tuple-element.16), channel_id=1, source_target_pairs={{0,16},{16,32},{32,48},{48,64},{64,80},{80,96},{96,112},{112,128},... | collective-permute-start | bytes 68 | tf_op jit(solution)/shard_map/ppermute | solution.py:20
  13.2 47.4 %all-to-all-start = ((s32[32,1,4]{2,1,0:T(1,128)}), s32[32,1,4]{2,1,0:T(1,128)S(1)}, u32[]{:S(2)}, u32[]{:S(2)}) async-start(s32[32,1,4]{2,1,0:T(1,128)} %bitcast.10), calls=%async_computation | async-start | bytes 32768 | tf_op jit(solution)/shard_map/all_to_all | solution.py:73
  44.8 5.9 %copy-start.1 = (bf16[2,5,2048]{2,0,1:T(2,128)(2,1)S(1)}, bf16[2,5,2048]{2,0,1:T(2,128)(2,1)}, u32[]{:S(2)}) copy-start(bf16[2,5,2048]{2,0,1:T(2,128)(2,1)} %param.4) | copy-start | bytes 122884
  52.8 4.7 %copy-start = (bf16[1,5,5,2048]{2,1,3,0:T(8,128)(2,1)S(1)}, bf16[1,5,5,2048]{2,1,3,0:T(8,128)(2,1)}, u32[]{:S(2)}) copy-start(bf16[1,5,5,2048]{2,1,3,0:T(8,128)(2,1)} %copy.82) | copy-start | bytes 307204
  52.8 4.7 %copy-start.2 = (f32[2048,2,5]{2,1,0:T(2,128)S(1)}, f32[2048,2,5]{2,1,0:T(2,128)}, u32[]{:S(2)}) copy-start(f32[2048,2,5]{2,1,0:T(2,128)} %fusion.4) | copy-start | bytes 245764
  63.0 17.3 %all-to-all-start.1 = ((bf16[2,5,32,4,128]{4,3,1,0,2:T(4,128)(2,1)}), bf16[2,5,32,4,128]{4,3,1,0,2:T(4,128)(2,1)S(1)}, u32[]{:S(2)}, u32[]{:S(2)}) async-start(bf16[2,5,32,4,128]{4,3,1,0,2:T(4,128)(2,1)} %copy.71), calls=%async_computation.1 | async-start | bytes 655360 | tf_op jit(solution)/shard_map/all_to_all | solution.py:82
  110.8 24.5 %all-to-all-start.2 = ((bf16[2,5,32,4,128]{4,3,1,0,2:T(4,128)(2,1)}), bf16[2,5,32,4,128]{4,3,1,0,2:T(4,128)(2,1)S(1)}, u32[]{:S(2)}, u32[]{:S(2)}) async-start(bf16[2,5,32,4,128]{4,3,1,0,2:T(4,128)(2,1)} %multiply_convert_fusion), calls=%async_computation.2 | async-start | bytes 655360 | tf_op jit(solution)/shard_map/all_to_all | solution.py:94
  136.5 5.5 %collective-permute-start.3 = (f32[2,5,1]{2,0,1:T(2,128)S(1)}, f32[2,5,1]{2,0,1:T(2,128)S(1)}, u32[]{:S(2)}, u32[]{:S(2)}) collective-permute-start(f32[2,5,1]{2,0,1:T(2,128)S(1)} %slice.51), channel_id=1, source_target_pairs={{0,16},{16,32},{32,48},{48,64},{64,80},{80,96},{96,112},{112,128},... | collective-permute-start | bytes 128 | tf_op jit(solution)/shard_map/ppermute | solution.py:32
  140.1 4.9 %collective-permute-start.2 = (f32[2,5,1]{2,0,1:T(2,128)S(1)}, f32[2,5,1]{2,0,1:T(2,128)S(1)}, u32[]{:S(2)}, u32[]{:S(2)}) collective-permute-start(f32[2,5,1]{2,0,1:T(2,128)S(1)} %slice.50), channel_id=1, source_target_pairs={{16,0},{32,16},{48,32},{64,48},{80,64},{96,80},{112,96},{128,112},... | collective-permute-start | bytes 128 | tf_op jit(solution)/shard_map/ppermute | solution.py:32
where the time goes:
time: 147 us; the launch traced here: 146 us
  starting transfers between devices  43 us (29%)
  local copies, waits for them, and re-layouts  36.5 us (25%)
  blocking collectives  29.3 us (20%)
  other arithmetic  20.2 us (14%)
  matrix products  13.6 us (9%)
  waiting for transfers between devices  3.01 us (2%)
    psum x1, blocking collectives, shards(): total_square = lax.psum(partial_square, 'mode')  29.3 us
    mul x3, other arithmetic, transpose_apply(): neighbor_link[None, :, :, :] * quadrature_weight[:, :, None, :]  15.3 us
    all_to_all x1, starting transfers between devices, shards(): lax.all_to_all(scaled, 'space', split_axis=2, concat_axis=2, tiled=True)  14.6 us
    mul x4, local copies, waits for them, and re-layouts, transpose_apply(): neighbor_link[None, :, :, :] * quadrature_weight[:, :, None, :]  14.4 us
    unnamed x10, local copies, waits for them, and re-layouts  14.1 us
    ppermute x1, starting transfers between devices, extended(): lax.ppermute(head, axis, [((i + 1) % count, i) for i in range(ends)])  8.77 us
    all_to_all x1, starting transfers between devices, shards(): lax.all_to_all(outgoing, 'space', split_axis=2, concat_axis=2, tiled=True)  7.39 us
    dot_general x1, matrix products, shards(): jnp.einsum('wvt,zvt->zwt', jacobian[0], basis, preferred_element_type=jnp...  5.87 us
  transfers between devices with their start and end apart: 7, of which 1 were waited for; matrix products, arithmetic and copies ran while one was open for 44% of the time, Pallas kernels for 0%

commit v1 on v0

v1 whole, which is shorter than its diff:
```python
import functools

import jax
import jax.numpy as jnp
from jax import lax
from jax.experimental import pallas as pl
from jax.experimental.pallas import tpu as pltpu
from jax.sharding import PartitionSpec as P

F = 5
PANEL = 32
TILE = 128
HALO_NEXT = 16
HALO_PREV = 23
ROWS = 24


def shifted(values, lane_shift):
    lane = lax.broadcasted_iota(jnp.int32, values.shape, 1)
    rolled = pltpu.roll(values, lane_shift % TILE, 1)
    carried = pltpu.roll(rolled, lane_shift % ROWS, 0)
    edge = 0 if lane_shift > 0 else TILE - 1
    return jnp.where(lane == edge, carried, rolled)


def split(values):
    high = values.astype(jnp.bfloat16)
    low = (values - high.astype(jnp.float32)).astype(jnp.bfloat16)
    return high, low


def kernel(
    spaces, modes, here,
    list_ref, weight_ref, basis_ref, jac_ref, out_ref,
    want_send, want, jac_rows, jac, basis_rows, basis, part_send, part, square, norm,
    send_sem, recv_sem,
):
    me = lax.axis_index("space")
    my_mode = lax.axis_index("mode")
    tiles = 16
    q_count = here * F

    def slot(j, q=None):
        return pl.ds(j * q_count, q_count) if q is None else pl.ds(j * q_count + q, 1)

    others = pl.ds(0, (spaces - 1) * q_count)

    def space_at(j):
        return lax.rem(me + 1 + j, spaces)

    def mode_at(j):
        return lax.rem(my_mode + 1 + j, modes)

    barrier = pltpu.get_barrier_semaphore()
    for j in range(spaces - 1):
        pl.semaphore_signal(barrier, inc=1, device_id={"space": space_at(j)})
    for j in range(modes - 1):
        pl.semaphore_signal(barrier, inc=1, device_id={"mode": mode_at(j)})

    row = lax.broadcasted_iota(jnp.int32, (spaces, TILE), 0)
    lane = lax.broadcasted_iota(jnp.int32, (spaces, TILE), 1)
    device = lax.rem(row + (me + 1), spaces)
    offset = jnp.where(lane < tiles + 1, lane, jnp.where(lane == HALO_PREV, -1, -(tiles * spaces + 1)))
    tile_id = device * tiles + offset
    wanted = jnp.zeros((spaces, TILE), jnp.float32)
    for entry in range(list_ref.shape[1]):
        wanted = wanted + jnp.where(tile_id == list_ref[0, entry], weight_ref[0, entry], 0.0)
    want_send[...] = wanted
    want[spaces - 1 :, :] = wanted[spaces - 1 :, :]

    for g in range(F):
        loaded = basis_ref[g].astype(jnp.float32)
        for k in range(tiles):
            basis_rows[g, 8 * k : 8 * k + here, :] = loaded[:, TILE * k : TILE * (k + 1)]
    for p in range(here):
        for g in range(F):
            basis[p * F + g, 0:tiles, :] = basis_rows[g, pl.ds(p, tiles, stride=8), :]

    pl.semaphore_wait(barrier, spaces - 1 + modes - 1)

    def send(src, dst, stage, **where):
        copy = pltpu.make_async_remote_copy(
            src_ref=src, dst_ref=dst, send_sem=send_sem.at[stage], recv_sem=recv_sem.at[stage],
            device_id=where,
        )
        copy.start()

    def arrived(ref, stage):
        pltpu.make_async_copy(ref, ref, recv_sem.at[stage]).wait()

    def left(ref, stage):
        pltpu.make_async_copy(ref, ref, send_sem.at[stage]).wait()

    following = space_at(0)
    previous = space_at(spaces - 2)
    send(basis.at[:, 15, :], basis.at[:, HALO_PREV, :], 0, space=following)
    send(basis.at[:, 0, :], basis.at[:, HALO_NEXT, :], 1, space=previous)
    for j in range(spaces - 1):
        send(want_send.at[pl.ds(j, 1)], want.at[pl.ds(spaces - 2 - j, 1)], 2, space=space_at(j))

    def spread(fg, carry):
        loaded = jac_ref[fg].astype(jnp.float32)
        for k in range(tiles):
            jac_rows[fg, 8 * k : 8 * k + 3, :] = loaded[:, TILE * k : TILE * (k + 1)]
        for w in range(3):
            jac[w * F * F + fg, 0:tiles, :] = jac_rows[fg, pl.ds(w, tiles, stride=8), :]
        return carry

    lax.fori_loop(0, F * F, spread, 0)

    arrived(basis.at[:, HALO_PREV, :], 0)
    arrived(basis.at[:, HALO_NEXT, :], 1)
    first = jnp.where(me == 0, 0.0, 1.0)
    last = jnp.where(me == spaces - 1, 0.0, 1.0)
    edge_row = lax.broadcasted_iota(jnp.int32, (ROWS, TILE), 0)
    keep = jnp.where(edge_row == HALO_PREV, first, jnp.where(edge_row == HALO_NEXT, last, 1.0))
    applied = []
    for p in range(here):
        total = [None] * F
        for g in range(F):
            centre = jnp.where(keep > 0, basis[p * F + g], 0.0)
            moved = (centre, shifted(centre, 1), shifted(centre, -1))
            for f in range(F):
                for w in range(3):
                    term = jac[w * F * F + f * F + g, 0:tiles, :] * moved[w][0:tiles]
                    total[f] = term if total[f] is None else total[f] + term
        applied += [t.astype(jnp.bfloat16) for t in total]
    field = jnp.concatenate(applied, axis=1)

    arrived(want.at[pl.ds(0, spaces - 1)], 2)
    weights = want[...]
    high, low = split(weights)
    partial = jnp.dot(
        jnp.concatenate([high[:, :tiles], low[:, :tiles]], axis=1),
        jnp.concatenate([field, field], axis=0),
        preferred_element_type=jnp.float32,
    )
    for q in range(q_count):
        part_send[pl.ds(q, spaces, stride=q_count), :] = partial[:, q * TILE : (q + 1) * TILE]
    for q in range(q_count):
        part[slot(spaces - 1, q), :] = partial[spaces - 1 :, q * TILE : (q + 1) * TILE]
    for j in range(spaces - 1):
        send(part_send.at[slot(j)], part.at[slot(spaces - 2 - j)], 3, space=space_at(j))
    send(jac.at[pl.ds(F * F, F * F), 0, :], jac.at[pl.ds(F * F, F * F), HALO_NEXT, :], 4, space=previous)
    send(jac.at[pl.ds(2 * F * F, F * F), 15, :], jac.at[pl.ds(2 * F * F, F * F), HALO_PREV, :], 5, space=following)

    turned = jnp.transpose(weights)[0:ROWS]
    turned_high, turned_low = split(turned)
    turned_all = jnp.concatenate([turned_high, turned_low, turned_high], axis=1)

    arrived(part.at[others], 3)
    rows = [
        jnp.sum(part[pl.ds(q, spaces, stride=q_count), :], axis=0, keepdims=True) for q in range(q_count)
    ]
    mine = sum(row * row for row in rows[1:]) + rows[0] * rows[0]
    square[modes - 1 :, :] = mine
    for j in range(modes - 1):
        send(square.at[pl.ds(modes - 1, 1)], square.at[pl.ds(modes - 2 - j, 1)], 6, mode=mode_at(j))
    arrived(square.at[pl.ds(0, modes - 1)], 6)
    mean = jnp.sum(square[...], axis=0, keepdims=True) / (PANEL * F)
    factor = lax.rsqrt(mean + 1e-5)
    for q in range(q_count):
        norm[slot(spaces - 1, q), :] = rows[q] * factor
    for j in range(spaces - 1):
        send(norm.at[slot(spaces - 1)], norm.at[slot(spaces - 2 - j)], 7, space=space_at(j))

    arrived(jac.at[pl.ds(F * F, F * F), HALO_NEXT, :], 4)
    arrived(jac.at[pl.ds(2 * F * F, F * F), HALO_PREV, :], 5)
    arrived(norm.at[others], 7)
    norm_high, norm_low = split(
        jnp.concatenate([norm[pl.ds(q, spaces, stride=q_count), :] for q in range(q_count)], axis=1)
    )
    returned = jnp.dot(
        turned_all,
        jnp.concatenate([norm_high, norm_high, norm_low], axis=0),
        preferred_element_type=jnp.float32,
    )
    for p in range(here):
        for f in range(F):
            parts = []
            for w in range(3):
                total = None
                for g in range(F):
                    q = p * F + g
                    term = jac[w * F * F + g * F + f] * returned[:, q * TILE : (q + 1) * TILE]
                    total = term if total is None else total + term
                parts.append(total)
            update = basis[p * F + f, 0:tiles, :] + parts[0][0:tiles]
            update = update + shifted(parts[1], -1)[0:tiles] + shifted(parts[2], 1)[0:tiles]
            out_ref[f, pl.ds(p, tiles, stride=here), :] = update

    left(basis.at[:, 15, :], 0)
    left(basis.at[:, 0, :], 1)
    left(want_send.at[pl.ds(0, spaces - 1)], 2)
    left(part_send.at[others], 3)
    left(jac.at[pl.ds(F * F, F * F), 0, :], 4)
    left(jac.at[pl.ds(2 * F * F, F * F), 15, :], 5)
    left(square.at[pl.ds(0, modes - 1)], 6)
    left(norm.at[others], 7)


def shards(spaces, modes, basis, jacobian, sample_list, sample_weight):
    here, fields, cells = basis.shape
    tiles = cells // TILE
    vmem = pl.BlockSpec(memory_space=pltpu.VMEM)
    smem = pl.BlockSpec(memory_space=pltpu.SMEM)
    update = pl.pallas_call(
        functools.partial(kernel, spaces, modes, here),
        out_shape=jax.ShapeDtypeStruct((fields, tiles * here, TILE), jnp.float32),
        in_specs=[smem, smem, vmem, vmem],
        out_specs=vmem,
        scratch_shapes=[
            pltpu.VMEM((spaces, TILE), jnp.float32),
            pltpu.VMEM((spaces, TILE), jnp.float32),
            pltpu.VMEM((fields * fields, 8 * tiles, TILE), jnp.float32),
            pltpu.VMEM((3 * fields * fields, ROWS, TILE), jnp.float32),
            pltpu.VMEM((fields, 8 * tiles, TILE), jnp.float32),
            pltpu.VMEM((here * fields, ROWS, TILE), jnp.float32),
            pltpu.VMEM((spaces * here * fields, TILE), jnp.float32),
            pltpu.VMEM((spaces * here * fields, TILE), jnp.float32),
            pltpu.VMEM((modes, TILE), jnp.float32),
            pltpu.VMEM((spaces * here * fields, TILE), jnp.float32),
            pltpu.SemaphoreType.DMA((8,)),
            pltpu.SemaphoreType.DMA((8,)),
        ],
        compiler_params=pltpu.CompilerParams(
            collective_id=0, has_side_effects=True, vmem_limit_bytes=24 * 2**20
        ),
    )(
        sample_list,
        sample_weight,
        basis.transpose(1, 0, 2),
        jacobian.transpose(1, 2, 0, 3).reshape(fields * fields, 3, cells),
    )
    update = update.reshape(fields, tiles, here, TILE).transpose(2, 0, 1, 3)
    return update.reshape(here, fields, cells)


def solution(mesh):
    placed = (
        P("mode", None, "space"),
        P(None, None, None, "space"),
        P("space", None),
        P("space", None),
    )
    return jax.shard_map(
        functools.partial(shards, mesh.shape["space"], mesh.shape["mode"]),
        mesh=mesh, in_specs=placed, out_specs=P("mode", None, "space"), check_vma=False,
    )
```

time: 147 us -> 43.4 us (0.30)
  starting transfers between devices: 43 us -> 0 us
  Pallas kernels: 0 us -> 40.1 us
  local copies, waits for them, and re-layouts: 36.5 us -> 3.09 us
  blocking collectives: 29.3 us -> 0 us
  other arithmetic: 20.2 us -> 0 us
  matrix products: 13.6 us -> 0 us
  waiting for transfers between devices: 3.01 us -> 0 us
    pallas_call x0 -> x1, Pallas kernels: none -> 40.1 us  [shards(): pl.pallas_call(functools.partial(kernel, spaces, modes, here), out_shape=...]
    psum x1 -> x0, blocking collectives: 29.3 us -> none  [shards(): total_square = lax.psum(partial_square, 'mode')]
    all_to_all x3 -> x0, starting transfers between devices: 26.8 us -> none  [the longest x1 14.6 us: shards(): lax.all_to_all(scaled, 'space', split_axis=2, concat_axis=2, tiled=True)]
    ppermute x4 -> x0, starting transfers between devices: 16.2 us -> none  [the longest x1 8.77 us: extended(): lax.ppermute(head, axis, [((i + 1) % count, i) for i in range(ends)])]
    mul x4 -> x0, other arithmetic: 15.3 us -> none  [the longest x3 15.3 us: transpose_apply(): neighbor_link[None, :, :, :] * quadrature_weight[:, :, None, :]]
    mul x5 -> x0, local copies, waits for them, and re-layouts: 14.5 us -> none  [the longest x4 14.4 us: transpose_apply(): neighbor_link[None, :, :, :] * quadrature_weight[:, :, None, :]]
    dot_general x6 -> x0, matrix products: 13.6 us -> none  [the longest x1 5.87 us: shards(): jnp.einsum('wvt,zvt->zwt', jacobian[0], basis, preferred_element_type=jnp...]
    unnamed x10 -> x9, local copies, waits for them, and re-layouts: 14.1 us -> 3.09 us
  transfers between devices with their start and end apart: 7 -> 0, of which waited for: 1 -> 0; matrix products, arithmetic and copies ran while one was open for 44% -> 0% of each run, Pallas kernels for 0% -> 0%
where the time goes in v1:
time: 43.4 us; the launch traced here: 43.2 us
  Pallas kernels  40.1 us (92%)
  local copies, waits for them, and re-layouts  3.09 us (7%)
    pallas_call x1, Pallas kernels, shards(): pl.pallas_call(functools.partial(kernel, spaces, modes, here), out_shape=...  40.1 us
    unnamed x9, local copies, waits for them, and re-layouts  3.09 us

profile of v1, /device:TPU:1, one launch (start us, length us, event | category | flops | bytes accessed | tf_op | source)
XLA Modules:
  0.0 43.2 jit_solution(10801865380134343625)
XLA Ops:
  0.0 0.0 copy-start.2
  0.0 0.0 copy-start.3
  0.0 0.7 %copy-done.2 = s32[1,64]{1,0:T(1,128)S(1)} copy-done((s32[1,64]{1,0:T(1,128)S(1)}, s32[1,64]{1,0:T(1,128)}, u32[]{:S(2)}) %copy-start.2) | copy-done | bytes 280
  0.7 0.0 copy-done.3
  0.7 0.0 copy-start
  0.7 1.0 %copy-done = bf16[3,5,5,2048]{3,0,2,1:T(4,128)(2,1)S(1)} copy-done((bf16[3,5,5,2048]{3,0,2,1:T(4,128)(2,1)S(1)}, bf16[3,5,5,2048]{3,0,2,1:T(4,128)(2,1)}, u32[]{:S(2)}) %copy-start) | copy-done | bytes 307224
  1.7 0.0 copy-start.1
  1.7 0.8 %copy-done.1 = bf16[2,5,2048]{2,0,1:T(2,128)(2,1)S(1)} copy-done((bf16[2,5,2048]{2,0,1:T(2,128)(2,1)S(1)}, bf16[2,5,2048]{2,0,1:T(2,128)(2,1)}, u32[]{:S(2)}) %copy-start.1) | copy-done | bytes 40984
  2.5 40.1 %shard_map.46 = f32[5,32,128]{2,1,0:T(8,128)S(1)} custom-call(s32[1,64]{1,0:T(1,128)S(1)} %copy-done.2, f32[1,64]{1,0:T(1,128)S(1)} %copy-done.3, bf16[5,2,2048]{2,1,0:T(2,128)(2,1)S(1)} %bitcast.11, bf16[25,3,2048]{2,1,0:T(4,128)(2,1)S(1)} %bitcast.9), custom_call_target="tpu_custom_call" | custom-call | tf_op jit(solution)/shard_map/pallas_call | solution.py:207
  42.5 0.6 %copy.7 = f32[2,5,2048]{2,0,1:T(2,128)} copy(f32[2,5,2048]{2,0,1:T(2,128)S(1)} %bitcast.10) | data formatting | bytes 163840
Async XLA Ops:
  0.0 0.7 %copy-start.2 = (s32[1,64]{1,0:T(1,128)S(1)}, s32[1,64]{1,0:T(1,128)}, u32[]{:S(2)}) copy-start(s32[1,64]{1,0:T(1,128)} %list_ref.1) | copy-start | bytes 772
  0.0 0.7 %copy-start.3 = (f32[1,64]{1,0:T(1,128)S(1)}, f32[1,64]{1,0:T(1,128)}, u32[]{:S(2)}) copy-start(f32[1,64]{1,0:T(1,128)} %weight_ref.1) | copy-start | bytes 772
  0.7 1.0 %copy-start = (bf16[3,5,5,2048]{3,0,2,1:T(4,128)(2,1)S(1)}, bf16[3,5,5,2048]{3,0,2,1:T(4,128)(2,1)}, u32[]{:S(2)}) copy-start(bf16[3,5,5,2048]{3,0,2,1:T(4,128)(2,1)} %param.5) | copy-start | bytes 921604
  1.7 0.8 %copy-start.1 = (bf16[2,5,2048]{2,0,1:T(2,128)(2,1)S(1)}, bf16[2,5,2048]{2,0,1:T(2,128)(2,1)}, u32[]{:S(2)}) copy-start(bf16[2,5,2048]{2,0,1:T(2,128)(2,1)} %param.4) | copy-start | bytes 122884
